TPU v7x, 32 devices: a whole 2x2x4 slice. The times are simulated.
32 devices in a mesh: dp: 2 (over x), seq: 16 (over z, y, core).
Axes of the slice: x: 2, y: 2, z: 4, core: 2. Of those that a mesh axis runs over, the one named last changes fastest.
Arguments:
- queries: bfloat16 [2, 16, 512, 1024], P('dp', 'seq'), may hold values from -16 to 16
- keys: bfloat16 [2, 16, 512, 1024], P('dp', 'seq'), may hold values from -12 to 12
- values: bfloat16 [2, 16, 512, 1024], P('dp', 'seq'), may hold values from -24 to 24
- out_proj: bfloat16 [1024, 2048], P(('dp', 'seq')), may hold values from -0.1875 to 0.1875
- out_grad: bfloat16 [2, 16, 512, 2048], P('dp', 'seq'), may hold values from -48 to 48
- block_pattern: int32 [4, 4], replicated, may hold values from 0 to 3, as said below
- col_offset: int32 [4], replicated, may hold values from 0 to 511
Outputs:
- layer_out: bfloat16 [2, 16, 512, 2048], P('dp', 'seq')
- q_grad: bfloat16 [2, 16, 512, 1024], P('dp', 'seq')
- k_grad: bfloat16 [2, 16, 512, 1024], P('dp', 'seq')
- v_grad: bfloat16 [2, 16, 512, 1024], P('dp', 'seq')
- w_grad: float32 [1024, 2048], P(('dp', 'seq'))
Inputs may be any that keep to these rules, and one draw needn't show every extreme that they name: `block_pattern`: for each row head, the entries name each of the 4 blocks of a grid row once, and entry j is never j.
All inputs are finite; a program needn't handle non-finite values.
Results may differ from a plain program's by a relative error of at most 0.006.
Values may be sent and summed in bfloat16 or wider, within the bound.
A program may use at most 128 MiB of HBM per device.

v0:
```python
import functools

import jax
import jax.numpy as jnp
from jax import lax
from jax.experimental import pallas as pl
from jax.experimental.pallas import tpu as pltpu
from jax.sharding import PartitionSpec as P

HD = 128
HR = 4
HC = 4
BLK = 128
NB = 4
HALF = HR * HD
CHUNKS = 4
SCALE = HD ** (-0.5)
NEG = -1e30
MESH = pl.DeviceIdType.MESH
F32 = jnp.float32
BF16 = jnp.bfloat16


def nt(a, b):
    return lax.dot_general(a, b, (((1,), (1,)), ((), ())), preferred_element_type=F32)


def nn(a, b):
    return jnp.dot(a, b, preferred_element_type=F32)


def tn(a, b):
    return lax.dot_general(a, b, (((0,), (0,)), ((), ())), preferred_element_type=F32)


def probs(query, key, bias):
    scores = nt(query, key) * SCALE + bias
    shifted = jnp.exp(scores - jnp.max(scores, axis=-1, keepdims=True))
    return shifted * (1.0 / jnp.sum(shifted, axis=-1, keepdims=True))


def score_grads(prob, grad, value):
    prob_grad = nt(grad, value)
    delta_sum = jnp.sum(prob * prob_grad, axis=-1, keepdims=True)
    return (prob * (prob_grad - delta_sum)).astype(BF16)


def head_cols(head_idx):
    return pl.ds(pl.multiple_of(head_idx * HD, HD), HD)


def body(seq, inside, q, k, v, w_in, og, pattern, offset, lo, dq, dk, dv, wg,
         w_all, grads, att, att_t, col_in, col_src, col_bias, col_prob, p_scr, s_scr,
         wp, core_in, keep, x_src, x_in, z_src, z_in,
         a_send, a_recv, g_send, g_recv, c_send, c_recv, x_send, x_recv, z_send, z_recv):
    tokens = q.shape[0]
    cols = tokens // seq
    width = og.shape[1]
    piece = width // CHUNKS
    pairs = seq // 2
    me = lax.axis_index("seq")
    dp = lax.axis_index("dp")
    core = lax.rem(me, 2)
    pair = me // 2
    y_at = lax.rem(pair, 2)
    z_at = pair // 2
    depth = seq // 4

    barrier = pltpu.get_barrier_semaphore()

    def greet(step, carry):
        pl.semaphore_signal(
            barrier, inc=1, device_id=(dp, lax.rem(me + step, seq)), device_id_type=MESH
        )
        return carry

    lax.fori_loop(1, seq, greet, 0)
    if inside:
        pl.semaphore_signal(barrier, inc=1, device_id=(1 - dp, me), device_id_type=MESH)
    pl.semaphore_wait(barrier, seq if inside else seq - 1)

    def push(src, dst, send, recv, target):
        pltpu.make_async_remote_copy(
            src_ref=src, dst_ref=dst, send_sem=send, recv_sem=recv,
            device_id=target, device_id_type=MESH,
        ).start()

    def drain(ref, sem):
        pltpu.make_async_copy(ref, ref, sem).wait()

    def col_rows(peer):
        return pl.ds(pl.multiple_of(peer * cols, cols), cols)

    def spread(source, slot):
        def one(step, carry):
            peer = lax.rem(me + step, seq)
            push(source(peer), col_in.at[slot, me], a_send.at[slot], a_recv.at[slot], (dp, peer))
            return carry

        lax.fori_loop(1, seq, one, 0)

    def arrived(slot):
        drain(col_in.at[slot, pl.ds(0, seq - 1)], a_recv.at[slot])

    def piece_cols(c):
        return pl.ds(pl.multiple_of(c * piece, piece), piece)

    if inside:
        w_all[dp, z_at, y_at, core] = w_in[...]
        for c in range(CHUNKS):
            def z_step(step, carry, c=c):
                z_to = lax.rem(z_at + step, depth)
                block = w_all.at[dp, z_at, y_at, core, :, piece_cols(c)]
                push(block, block, g_send.at[0, c], g_recv.at[0, c],
                     (dp, (z_to * 2 + y_at) * 2 + core))
                return carry

            lax.fori_loop(1, depth, z_step, 0)
        weights = w_all
    else:
        weights = w_in

    spread(lambda peer: q.at[col_rows(peer), pl.ds(HALF, HALF)], 0)
    col_in[0, me] = q[col_rows(me), HALF:]

    row_at = lax.broadcasted_iota(jnp.int32, (tokens, tokens), 0)
    lane_at = lax.broadcasted_iota(jnp.int32, (tokens, tokens), 1)

    def moved(tensor, head_idx, forth):
        apart = (row_at - lane_at if forth else lane_at - row_at) - offset[head_idx]
        chosen = jnp.where((apart == 0) | (apart == -tokens), 1.0, 0.0).astype(BF16)
        return nn(chosen, tensor).astype(BF16)

    for tensor, src_slot, slot in ((k, 0, 1), (v, 1, 2)):
        for head_idx in range(HC):
            shifted = moved(tensor[:, HALF + head_idx * HD:HALF + (head_idx + 1) * HD], head_idx, True)
            col_src[src_slot, :, :, head_idx * HD:(head_idx + 1) * HD] = shifted.reshape(seq, cols, HD)
        spread(lambda peer, s=src_slot: col_src.at[s, peer], slot)
        col_in[slot, me] = col_src[src_slot, me]

    part_row = lax.broadcasted_iota(jnp.int32, (BLK, tokens), 0)
    part_lane = lax.broadcasted_iota(jnp.int32, (BLK, tokens), 1)
    col_bias[...] = jnp.where(lax.rem(part_row, cols) == lax.rem(part_lane, cols), 0.0, NEG)

    if inside:
        for c in range(CHUNKS):
            drain(w_all.at[0, pl.ds(0, depth - 1), 0, 0, :, piece_cols(c)], g_recv.at[0, c])
            block = w_all.at[dp, :, y_at, core, :, piece_cols(c)]
            push(block, block, g_send.at[1, c], g_recv.at[1, c],
                 (dp, (z_at * 2 + 1 - y_at) * 2 + core))
        for c in range(CHUNKS):
            drain(w_all.at[0, :, 0, 0, :, piece_cols(c)], g_recv.at[1, c])
            block = w_all.at[dp, :, :, core, :, piece_cols(c)]
            push(block, block, g_send.at[2, c], g_recv.at[2, c], (1 - dp, me))
        for c in range(CHUNKS):
            drain(w_all.at[0, :, :, 0, :, piece_cols(c)], g_recv.at[2, c])
            block = w_all.at[:, :, :, core, :, piece_cols(c)]
            push(block, block, g_send.at[3, c], g_recv.at[3, c], (dp, pair * 2 + 1 - core))
        for c in range(CHUNKS):
            drain(w_all.at[:, :, :, 0, :, piece_cols(c)], g_recv.at[3, c])

    tall = 256
    steps = tall // (4 * weights.shape[4])

    def attn_grad(half):
        def one(n, carry):
            rows = weights[half, pl.ds(n * steps, steps)].reshape(tall, width)
            part = nt(og[...], rows).astype(BF16)
            grads[:, pl.ds(pl.multiple_of(half * HALF + n * tall, tall), tall)] = part
            return carry

        lax.fori_loop(0, HALF // tall, one, 0)

    attn_grad(1)
    spread(lambda peer: grads.at[col_rows(peer), pl.ds(HALF, HALF)], 3)
    col_in[3, me] = grads[col_rows(me), HALF:]

    part_slots = BLK // cols

    def col_block(ref, slot, part, where):
        return ref[slot, part * part_slots:(part + 1) * part_slots, :, where].reshape(BLK, HD)

    def col_full(ref, slot, where):
        return ref[slot, :, :, where].reshape(tokens, HD)

    def col_put(slot, part, where, val):
        col_src[slot, part * part_slots:(part + 1) * part_slots, :, where] = (
            val.astype(BF16).reshape(part_slots, cols, HD))

    parts = tokens // BLK
    arrived(0)
    arrived(1)
    arrived(2)

    def col_forward(head_idx, carry):
        where = head_cols(head_idx)
        key, value = col_full(col_in, 1, where), col_full(col_in, 2, where)
        for part in range(parts):
            prob = probs(col_block(col_in, 0, part, where), key, col_bias[...])
            col_prob[head_idx, part * BLK:(part + 1) * BLK] = prob
            col_put(2, part, where, nn(prob.astype(BF16), value))
        return carry

    lax.fori_loop(0, HC, col_forward, 0)
    spread(lambda peer: col_src.at[2, peer], 4)
    col_in[4, me] = col_src[2, me]

    attn_grad(0)
    key_block = lax.broadcasted_iota(jnp.int32, (1, tokens), 1) // BLK

    def row_head(head_idx, carry):
        where = head_cols(head_idx)
        key, value = k[:, where], v[:, where]
        for part in range(parts):
            rows = slice(part * BLK, (part + 1) * BLK)
            seen = (key_block == part) | (key_block == pattern[head_idx, part])
            prob = probs(q[rows, where], key, jnp.where(seen, 0.0, NEG))
            half_prob = prob.astype(BF16)
            att[rows, where] = nn(half_prob, value).astype(BF16)
            score_grad = score_grads(prob, grads[rows, where], value)
            dq[rows, where] = (nn(score_grad, key) * SCALE).astype(BF16)
            p_scr[rows] = half_prob
            s_scr[rows] = score_grad
        dk[:, where] = (tn(s_scr[...], q[:, where]) * SCALE).astype(BF16)
        dv[:, where] = tn(p_scr[...], grads[:, where]).astype(BF16)
        return carry

    lax.fori_loop(0, HR, row_head, 0)

    def w_part(half):
        att_t[...] = att[:, half * HALF:(half + 1) * HALF].astype(F32).T.astype(BF16)

        def one(c, carry):
            at = piece_cols(c)
            product = nn(att_t[...], og[:, at])
            if inside:
                wp[half, :, :, :, at] = product.astype(BF16).reshape(pairs, 2, HALF // seq, piece)
                push(wp.at[half, :, 1 - core, :, at], core_in.at[half, :, :, at],
                     c_send.at[half, c], c_recv.at[half, c], (dp, pair * 2 + 1 - core))
            else:
                wg[pl.ds(half * HALF, HALF), at] = product
            return carry

        lax.fori_loop(0, CHUNKS, one, 0)

    w_part(0)

    arrived(3)

    def col_backward(head_idx, carry):
        where = head_cols(head_idx)
        key, value = col_full(col_in, 1, where), col_full(col_in, 2, where)
        for part in range(parts):
            rows = slice(part * BLK, (part + 1) * BLK)
            prob = col_prob[head_idx, rows]
            score_grad = score_grads(prob, col_block(col_in, 3, part, where), value)
            col_put(3, part, where, nn(score_grad, key) * SCALE)
            p_scr[rows] = prob.astype(BF16)
            s_scr[rows] = score_grad
        key_grad = tn(s_scr[...], col_full(col_in, 0, where)) * SCALE
        value_grad = tn(p_scr[...], col_full(col_in, 3, where))
        col_src[4, :, :, where] = key_grad.astype(BF16).reshape(seq, cols, HD)
        col_src[5, :, :, where] = value_grad.astype(BF16).reshape(seq, cols, HD)
        return carry

    lax.fori_loop(0, HC, col_backward, 0)

    arrived(4)
    att[:, HALF:] = col_in[4].reshape(tokens, HALF)
    w_part(1)
    for slot in (5, 6, 7):
        spread(lambda peer, s=slot - 2: col_src.at[s, peer], slot)
        col_in[slot, me] = col_src[slot - 2, me]

    if inside:
        def x_step(c, carry):
            at = piece_cols(c)
            for half in (0, 1):
                drain(core_in.at[half, :, :, at], c_recv.at[half, c])
            keep[:, :, at] = wp[dp, :, core, :, at].astype(F32) + core_in[dp, :, :, at].astype(F32)
            x_src[:, :, at] = (
                wp[1 - dp, :, core, :, at].astype(F32) + core_in[1 - dp, :, :, at].astype(F32)
            ).astype(BF16)
            push(x_src.at[:, :, at], x_in.at[:, :, at], x_send.at[c], x_recv.at[c], (1 - dp, me))
            return carry

        lax.fori_loop(0, CHUNKS, x_step, 0)

    def layer(n, carry):
        at = pl.ds(pl.multiple_of(n * tall, tall), tall)
        lo[:, at] = nn(att[...], weights[:, :, :, :, :, at].reshape(2 * HALF, tall)).astype(BF16)
        return carry

    lax.fori_loop(0, width // tall, layer, 0)

    if inside:
        def z_step(c, carry):
            at = piece_cols(c)
            drain(x_in.at[:, :, at], x_recv.at[c])
            z_src[:, :, at] = (keep[:, :, at] + x_in[:, :, at].astype(F32)).astype(BF16)
            z_in[pair, :, at] = z_src[pair, :, at]

            def one(step, inner):
                peer = lax.rem(pair + step, pairs)
                push(z_src.at[peer, :, at], z_in.at[pair, :, at], z_send.at[c], z_recv.at[c],
                     (dp, peer * 2 + core))
                return inner

            lax.fori_loop(1, pairs, one, 0)
            return carry

        lax.fori_loop(0, CHUNKS, z_step, 0)

    arrived(5)
    dq[:, HALF:] = col_in[5].reshape(tokens, HALF)
    for slot, target in ((6, dk), (7, dv)):
        arrived(slot)
        for head_idx in range(HC):
            lanes = slice(head_idx * HD, (head_idx + 1) * HD)
            back = moved(col_in[slot, :, :, lanes].reshape(tokens, HD), head_idx, False)
            target[:, HALF + head_idx * HD:HALF + (head_idx + 1) * HD] = back

    if inside:
        factor = (2 * seq * tokens) ** (-0.5)
        for c in range(CHUNKS):
            at = piece_cols(c)
            drain(z_in.at[pl.ds(0, pairs - 1), :, at], z_recv.at[c])
            wg[:, at] = jnp.sum(z_in[:, :, at].astype(F32), axis=0) * factor
        for c in range(CHUNKS):
            drain(w_all.at[0, pl.ds(0, depth - 1), 0, 0, :, piece_cols(c)], g_send.at[0, c])
            drain(w_all.at[0, :, 0, 0, :, piece_cols(c)], g_send.at[1, c])
            drain(w_all.at[0, :, :, 0, :, piece_cols(c)], g_send.at[2, c])
            drain(w_all.at[:, :, :, 0, :, piece_cols(c)], g_send.at[3, c])
            for half in (0, 1):
                drain(core_in.at[half, :, :, piece_cols(c)], c_send.at[half, c])
            drain(x_in.at[:, :, piece_cols(c)], x_send.at[c])
            drain(z_in.at[pl.ds(0, pairs - 1), :, piece_cols(c)], z_send.at[c])
    for slot in range(8):
        drain(col_in.at[slot, pl.ds(0, seq - 1)], a_send.at[slot])


def shards(dp_count, seq, queries, keys, values, out_proj, out_grad, block_pattern, col_offset):
    tokens, feats = queries.shape[2:]
    width = out_grad.shape[3]
    share = out_proj.shape[0]
    cols = tokens // seq
    inside = dp_count == 2 and share % 16 == 0
    split = (2, seq // 4, 2, 2, feats // (2 * seq), width)
    if inside:
        w_in = out_proj
    else:
        w_in = lax.all_gather(out_proj, ("dp", "seq"), axis=0, tiled=True).reshape(split)
    small = lambda shape, kind: pltpu.VMEM(shape if inside else (16, 128), kind)
    group = (seq // 2, share, width)
    sems = pltpu.SemaphoreType.DMA
    vmem = pl.BlockSpec(memory_space=pltpu.VMEM)
    smem = pl.BlockSpec(memory_space=pltpu.SMEM)
    flat = jax.ShapeDtypeStruct((tokens, feats), BF16)
    outs = pl.pallas_call(
        functools.partial(body, seq, inside),
        out_shape=[
            jax.ShapeDtypeStruct((tokens, width), BF16), flat, flat, flat,
            jax.ShapeDtypeStruct((share if inside else feats, width), F32),
        ],
        in_specs=[vmem] * 5 + [smem] * 2,
        out_specs=[vmem] * 5,
        scratch_shapes=[
            small(split, BF16),
            pltpu.VMEM((tokens, feats), BF16),
            pltpu.VMEM((tokens, feats), BF16),
            pltpu.VMEM((HALF, tokens), BF16),
            pltpu.VMEM((8, seq, cols, HALF), BF16),
            pltpu.VMEM((6, seq, cols, HALF), BF16),
            pltpu.VMEM((BLK, tokens), F32),
            pltpu.VMEM((HC, tokens, tokens), F32),
            pltpu.VMEM((tokens, tokens), BF16),
            pltpu.VMEM((tokens, tokens), BF16),
            small((2, seq // 2, 2, share, width), BF16),
            small((2,) + group, BF16),
            small(group, F32),
            small(group, BF16),
            small(group, BF16),
            small(group, BF16),
            small(group, BF16),
            sems((8,)), sems((8,)),
            sems((4, CHUNKS)), sems((4, CHUNKS)),
            sems((2, CHUNKS)), sems((2, CHUNKS)),
            sems((CHUNKS,)), sems((CHUNKS,)),
            sems((CHUNKS,)), sems((CHUNKS,)),
        ],
        compiler_params=pltpu.CompilerParams(
            collective_id=0, has_side_effects=True, vmem_limit_bytes=58 * 2 ** 20
        ),
        cost_estimate=pl.CostEstimate(
            flops=12 * 10 ** 9, bytes_accessed=11 * 2 ** 20, transcendentals=2 * 2 ** 20
        ),
    )(
        queries.reshape(tokens, feats), keys.reshape(tokens, feats), values.reshape(tokens, feats),
        w_in, out_grad.reshape(tokens, width), block_pattern, col_offset,
    )
    layer_out, q_grad, k_grad, v_grad, w_grad = outs
    if not inside:
        w_grad = lax.psum_scatter(w_grad, ("dp", "seq"), scatter_dimension=0, tiled=True)
        w_grad = w_grad * (dp_count * seq * tokens) ** (-0.5)
    shape = (1, 1, tokens, feats)
    return (
        layer_out.reshape(1, 1, tokens, width),
        q_grad.reshape(shape), k_grad.reshape(shape), v_grad.reshape(shape), w_grad,
    )


def solution(mesh):
    rows = P("dp", "seq", None, None)
    flat = P(("dp", "seq"), None)
    in_specs = (rows, rows, rows, flat, rows, P(), P())
    out_specs = (rows, rows, rows, rows, flat)
    return jax.shard_map(
        functools.partial(shards, mesh.shape["dp"], mesh.shape["seq"]),
        mesh=mesh, in_specs=in_specs, out_specs=out_specs, check_vma=False,
    )
```

profile of v0, /device:TPU:26, one launch (start us, length us, event | category | flops | bytes accessed | tf_op | source)
XLA Modules:
  0.0 158.2 jit_solution(17056064984129431146)
XLA Ops:
  0.6 150.1 %shard_map.110 = (bf16[512,2048]{1,0:T(8,128)(2,1)}, bf16[512,1024]{1,0:T(8,128)(2,1)}, bf16[512,1024]{1,0:T(8,128)(2,1)}, bf16[512,1024]{1,0:T(8,128)(2,1)}, f32[32,2048]{1,0:T(8,128)}) custom-call(bf16[512,1024]{1,0:T(8,128)(2,1)} %bitcast.13, bf16[512,1024]{1,0:T(8,128)(2,1)} %bitcast.14, bf16[512,1024]{1,0:T(8,128)(2,1)} %bitcast.15, ...), custom_call_target="tpu_custom_call" | custom-call | flops 12000000000 | bytes 11534336 | tf_op jit(solution)/shard_map/pallas_call | solution.py:359
  150.7 0.0 copy-start.2
  150.7 3.2 %copy.17 = bf16[1,1,512,2048]{3,2,1,0:T(8,128)(2,1)} copy(bf16[1,1,512,2048]{3,2,1,0:T(8,128)(2,1)} %bitcast.8) | data formatting | bytes 4194304
  154.0 0.0 copy-done.2
  154.0 0.0 copy-start.1
  154.0 0.0 copy-start
  154.0 1.0 copy.18
  155.0 0.6 copy-done.1
  155.6 0.0 copy-start.3
  155.6 1.0 copy.19
  156.6 0.0 copy-done
  156.6 1.0 copy.20
  157.5 0.0 copy-done.3
  157.5 0.7 copy.21
Async XLA Ops:
  150.7 3.3 %copy-start.2 = (bf16[512,1024]{1,0:T(8,128)(2,1)S(1)}, bf16[512,1024]{1,0:T(8,128)(2,1)}, u32[]{:S(2)}) copy-start(bf16[512,1024]{1,0:T(8,128)(2,1)} %get-tuple-element.11) | copy-start | bytes 3145732
  154.0 1.6 %copy-start.1 = (bf16[512,1024]{1,0:T(8,128)(2,1)S(1)}, bf16[512,1024]{1,0:T(8,128)(2,1)}, u32[]{:S(2)}) copy-start(bf16[512,1024]{1,0:T(8,128)(2,1)} %get-tuple-element.12) | copy-start | bytes 3145732
  154.0 2.6 %copy-start = (bf16[512,1024]{1,0:T(8,128)(2,1)S(1)}, bf16[512,1024]{1,0:T(8,128)(2,1)}, u32[]{:S(2)}) copy-start(bf16[512,1024]{1,0:T(8,128)(2,1)} %get-tuple-element.13) | copy-start | bytes 3145732
  155.6 1.9 %copy-start.3 = (f32[32,2048]{1,0:T(8,128)S(1)}, f32[32,2048]{1,0:T(8,128)}, u32[]{:S(2)}) copy-start(f32[32,2048]{1,0:T(8,128)} %get-tuple-element.24) | copy-start | bytes 786436
where the time goes:
time: 158 us
  Pallas kernels  150 us (95%)
  local copies, waits for them, and re-layouts  7.5 us (5%)
    pallas_call x1, Pallas kernels, shards(): pl.pallas_call(functools.partial(body, seq, inside), out_shape=[jax.Shape...  150 us
    unnamed x13, local copies, waits for them, and re-layouts  7.5 us

commit v1 on v0

--- a/solution.py
+++ b/solution.py
@@ -49,15 +49,14 @@
     return pl.ds(pl.multiple_of(head_idx * HD, HD), HD)
 
 
-def body(seq, inside, q, k, v, w_in, og, pattern, offset, lo, dq, dk, dv, wg,
-         w_all, grads, att, att_t, col_in, col_src, col_bias, col_prob, p_scr, s_scr,
-         wp, core_in, keep, x_src, x_in, z_src, z_in,
-         a_send, a_recv, g_send, g_recv, c_send, c_recv, x_send, x_recv, z_send, z_recv):
+def body(seq, inside, q_far, k_far, v_far, w_far, og_far, pattern, offset, lo, dq, dk, dv, wg,
+         q, k, v, w_in, og, l_sem, w_all, grads, att, att_t, col_in, col_src, col_bias, col_prob, p_scr, s_scr,
+         wp, core_in, y_src, y_in, keep, x_src, x_in, z_src, z_in,
+         a_send, a_recv, g_send, g_recv, c_send, c_recv, y_send, y_recv, x_send, x_recv, z_send, z_recv):
     tokens = q.shape[0]
     cols = tokens // seq
     width = og.shape[1]
     piece = width // CHUNKS
-    pairs = seq // 2
     me = lax.axis_index("seq")
     dp = lax.axis_index("dp")
     core = lax.rem(me, 2)
@@ -66,6 +65,11 @@
     z_at = pair // 2
     depth = seq // 4
 
+    near = [pltpu.make_async_copy(far, close, l_sem.at[at]) for at, (far, close) in enumerate(
+        ((w_far, w_in), (k_far, k), (q_far, q), (v_far, v), (og_far, og)))]
+    for load in near:
+        load.start()
+
     barrier = pltpu.get_barrier_semaphore()
 
     def greet(step, carry):
@@ -105,6 +109,7 @@
     def piece_cols(c):
         return pl.ds(pl.multiple_of(c * piece, piece), piece)
 
+    near[0].wait()
     if inside:
         w_all[dp, z_at, y_at, core] = w_in[...]
         for c in range(CHUNKS):
@@ -120,9 +125,6 @@
     else:
         weights = w_in
 
-    spread(lambda peer: q.at[col_rows(peer), pl.ds(HALF, HALF)], 0)
-    col_in[0, me] = q[col_rows(me), HALF:]
-
     row_at = lax.broadcasted_iota(jnp.int32, (tokens, tokens), 0)
     lane_at = lax.broadcasted_iota(jnp.int32, (tokens, tokens), 1)
 
@@ -131,12 +133,17 @@
         chosen = jnp.where((apart == 0) | (apart == -tokens), 1.0, 0.0).astype(BF16)
         return nn(chosen, tensor).astype(BF16)
 
-    for tensor, src_slot, slot in ((k, 0, 1), (v, 1, 2)):
+    def move_all(tensor, src_slot):
         for head_idx in range(HC):
             shifted = moved(tensor[:, HALF + head_idx * HD:HALF + (head_idx + 1) * HD], head_idx, True)
             col_src[src_slot, :, :, head_idx * HD:(head_idx + 1) * HD] = shifted.reshape(seq, cols, HD)
-        spread(lambda peer, s=src_slot: col_src.at[s, peer], slot)
+
+    def spread_moved(src_slot, slot):
+        spread(lambda peer: col_src.at[src_slot, peer], slot)
         col_in[slot, me] = col_src[src_slot, me]
+
+    near[1].wait()
+    move_all(k, 0)
 
     part_row = lax.broadcasted_iota(jnp.int32, (BLK, tokens), 0)
     part_lane = lax.broadcasted_iota(jnp.int32, (BLK, tokens), 1)
@@ -148,16 +155,26 @@
             block = w_all.at[dp, :, y_at, core, :, piece_cols(c)]
             push(block, block, g_send.at[1, c], g_recv.at[1, c],
                  (dp, (z_at * 2 + 1 - y_at) * 2 + core))
+    near[2].wait()
+    spread(lambda peer: q.at[col_rows(peer), pl.ds(HALF, HALF)], 0)
+    col_in[0, me] = q[col_rows(me), HALF:]
+    spread_moved(0, 1)
+    near[3].wait()
+    move_all(v, 1)
+    if inside:
         for c in range(CHUNKS):
             drain(w_all.at[0, :, 0, 0, :, piece_cols(c)], g_recv.at[1, c])
             block = w_all.at[dp, :, :, core, :, piece_cols(c)]
             push(block, block, g_send.at[2, c], g_recv.at[2, c], (1 - dp, me))
+    spread_moved(1, 2)
+    if inside:
         for c in range(CHUNKS):
             drain(w_all.at[0, :, :, 0, :, piece_cols(c)], g_recv.at[2, c])
             block = w_all.at[:, :, :, core, :, piece_cols(c)]
             push(block, block, g_send.at[3, c], g_recv.at[3, c], (dp, pair * 2 + 1 - core))
         for c in range(CHUNKS):
             drain(w_all.at[:, :, :, 0, :, piece_cols(c)], g_recv.at[3, c])
+    near[4].wait()
 
     tall = 256
     steps = tall // (4 * weights.shape[4])
@@ -225,7 +242,7 @@
         dv[:, where] = tn(p_scr[...], grads[:, where]).astype(BF16)
         return carry
 
-    lax.fori_loop(0, HR, row_head, 0)
+    lax.fori_loop(0, HR // 2, row_head, 0)
 
     def w_part(half):
         att_t[...] = att[:, half * HALF:(half + 1) * HALF].astype(F32).T.astype(BF16)
@@ -234,8 +251,9 @@
             at = piece_cols(c)
             product = nn(att_t[...], og[:, at])
             if inside:
-                wp[half, :, :, :, at] = product.astype(BF16).reshape(pairs, 2, HALF // seq, piece)
-                push(wp.at[half, :, 1 - core, :, at], core_in.at[half, :, :, at],
+                wp[half, :, :, :, :, at] = product.astype(BF16).reshape(
+                    depth, 2, 2, HALF // seq, piece)
+                push(wp.at[half, :, :, 1 - core, :, at], core_in.at[half, :, :, :, at],
                      c_send.at[half, c], c_recv.at[half, c], (dp, pair * 2 + 1 - core))
             else:
                 wg[pl.ds(half * HALF, HALF), at] = product
@@ -243,7 +261,21 @@
 
         lax.fori_loop(0, CHUNKS, one, 0)
 
-    w_part(0)
+    def y_part(half):
+        def one(c, carry):
+            at = piece_cols(c)
+            drain(core_in.at[half, :, :, :, at], c_recv.at[half, c])
+            other = 1 - y_at
+            y_src[half, :, :, at] = (
+                wp[half, :, other, core, :, at].astype(F32) + core_in[half, :, other, :, at].astype(F32)
+            ).astype(BF16)
+            keep[half, :, :, at] = (
+                wp[half, :, y_at, core, :, at].astype(F32) + core_in[half, :, y_at, :, at].astype(F32))
+            push(y_src.at[half, :, :, at], y_in.at[half, :, :, at], y_send.at[half, c],
+                 y_recv.at[half, c], (dp, (z_at * 2 + other) * 2 + core))
+            return carry
+
+        lax.fori_loop(0, CHUNKS, one, 0)
 
     arrived(3)
 
@@ -265,22 +297,24 @@
 
     lax.fori_loop(0, HC, col_backward, 0)
 
+    for slot in (5, 6, 7):
+        spread_moved(slot - 2, slot)
+    lax.fori_loop(HR // 2, HR, row_head, 0)
+    w_part(0)
+    if inside:
+        y_part(0)
     arrived(4)
     att[:, HALF:] = col_in[4].reshape(tokens, HALF)
     w_part(1)
-    for slot in (5, 6, 7):
-        spread(lambda peer, s=slot - 2: col_src.at[s, peer], slot)
-        col_in[slot, me] = col_src[slot - 2, me]
-
-    if inside:
+    if inside:
+        y_part(1)
+
         def x_step(c, carry):
             at = piece_cols(c)
             for half in (0, 1):
-                drain(core_in.at[half, :, :, at], c_recv.at[half, c])
-            keep[:, :, at] = wp[dp, :, core, :, at].astype(F32) + core_in[dp, :, :, at].astype(F32)
+                drain(y_in.at[half, :, :, at], y_recv.at[half, c])
             x_src[:, :, at] = (
-                wp[1 - dp, :, core, :, at].astype(F32) + core_in[1 - dp, :, :, at].astype(F32)
-            ).astype(BF16)
+                keep[1 - dp, :, :, at] + y_in[1 - dp, :, :, at].astype(F32)).astype(BF16)
             push(x_src.at[:, :, at], x_in.at[:, :, at], x_send.at[c], x_recv.at[c], (1 - dp, me))
             return carry
 
@@ -297,16 +331,18 @@
         def z_step(c, carry):
             at = piece_cols(c)
             drain(x_in.at[:, :, at], x_recv.at[c])
-            z_src[:, :, at] = (keep[:, :, at] + x_in[:, :, at].astype(F32)).astype(BF16)
-            z_in[pair, :, at] = z_src[pair, :, at]
+            z_src[:, :, at] = (
+                keep[dp, :, :, at] + y_in[dp, :, :, at].astype(F32) + x_in[:, :, at].astype(F32)
+            ).astype(BF16)
+            z_in[z_at, :, at] = z_src[z_at, :, at]
 
             def one(step, inner):
-                peer = lax.rem(pair + step, pairs)
-                push(z_src.at[peer, :, at], z_in.at[pair, :, at], z_send.at[c], z_recv.at[c],
-                     (dp, peer * 2 + core))
+                peer = lax.rem(z_at + step, depth)
+                push(z_src.at[peer, :, at], z_in.at[z_at, :, at], z_send.at[c], z_recv.at[c],
+                     (dp, (peer * 2 + y_at) * 2 + core))
                 return inner
 
-            lax.fori_loop(1, pairs, one, 0)
+            lax.fori_loop(1, depth, one, 0)
             return carry
 
         lax.fori_loop(0, CHUNKS, z_step, 0)
@@ -324,7 +360,7 @@
         factor = (2 * seq * tokens) ** (-0.5)
         for c in range(CHUNKS):
             at = piece_cols(c)
-            drain(z_in.at[pl.ds(0, pairs - 1), :, at], z_recv.at[c])
+            drain(z_in.at[pl.ds(0, depth - 1), :, at], z_recv.at[c])
             wg[:, at] = jnp.sum(z_in[:, :, at].astype(F32), axis=0) * factor
         for c in range(CHUNKS):
             drain(w_all.at[0, pl.ds(0, depth - 1), 0, 0, :, piece_cols(c)], g_send.at[0, c])
@@ -332,11 +368,27 @@
             drain(w_all.at[0, :, :, 0, :, piece_cols(c)], g_send.at[2, c])
             drain(w_all.at[:, :, :, 0, :, piece_cols(c)], g_send.at[3, c])
             for half in (0, 1):
-                drain(core_in.at[half, :, :, piece_cols(c)], c_send.at[half, c])
+                drain(core_in.at[half, :, :, :, piece_cols(c)], c_send.at[half, c])
+                drain(y_in.at[half, :, :, piece_cols(c)], y_send.at[half, c])
             drain(x_in.at[:, :, piece_cols(c)], x_send.at[c])
-            drain(z_in.at[pl.ds(0, pairs - 1), :, piece_cols(c)], z_send.at[c])
+            drain(z_in.at[pl.ds(0, depth - 1), :, piece_cols(c)], z_send.at[c])
     for slot in range(8):
         drain(col_in.at[slot, pl.ds(0, seq - 1)], a_send.at[slot])
+
+
+def deliver(*refs):
+    sources, targets, sem = refs[:5], refs[5:10], refs[10]
+    copies = []
+    for at, (source, target) in enumerate(zip(sources, targets)):
+        cuts = 4 if source.shape[0] >= 64 else 1
+        rows = source.shape[0] // cuts
+        for cut in range(cuts):
+            part = pl.ds(cut * rows, rows)
+            copies.append(pltpu.make_async_copy(source.at[part], target.at[part], sem.at[at, cut]))
+    for copy in copies:
+        copy.start()
+    for copy in copies:
+        copy.wait()
 
 
 def shards(dp_count, seq, queries, keys, values, out_proj, out_grad, block_pattern, col_offset):
@@ -351,7 +403,7 @@
     else:
         w_in = lax.all_gather(out_proj, ("dp", "seq"), axis=0, tiled=True).reshape(split)
     small = lambda shape, kind: pltpu.VMEM(shape if inside else (16, 128), kind)
-    group = (seq // 2, share, width)
+    group = (seq // 4, share, width)
     sems = pltpu.SemaphoreType.DMA
     vmem = pl.BlockSpec(memory_space=pltpu.VMEM)
     smem = pl.BlockSpec(memory_space=pltpu.SMEM)
@@ -362,9 +414,15 @@
             jax.ShapeDtypeStruct((tokens, width), BF16), flat, flat, flat,
             jax.ShapeDtypeStruct((share if inside else feats, width), F32),
         ],
-        in_specs=[vmem] * 5 + [smem] * 2,
+        in_specs=[pl.BlockSpec(memory_space=pl.ANY)] * 5 + [smem] * 2,
         out_specs=[vmem] * 5,
         scratch_shapes=[
+            pltpu.VMEM((tokens, feats), BF16),
+            pltpu.VMEM((tokens, feats), BF16),
+            pltpu.VMEM((tokens, feats), BF16),
+            pltpu.VMEM(w_in.shape, BF16),
+            pltpu.VMEM((tokens, width), BF16),
+            sems((5,)),
             small(split, BF16),
             pltpu.VMEM((tokens, feats), BF16),
             pltpu.VMEM((tokens, feats), BF16),
@@ -375,15 +433,18 @@
             pltpu.VMEM((HC, tokens, tokens), F32),
             pltpu.VMEM((tokens, tokens), BF16),
             pltpu.VMEM((tokens, tokens), BF16),
-            small((2, seq // 2, 2, share, width), BF16),
+            small((2, seq // 4, 2, 2, share, width), BF16),
+            small((2, seq // 4, 2, share, width), BF16),
             small((2,) + group, BF16),
-            small(group, F32),
+            small((2,) + group, BF16),
+            small((2,) + group, F32),
             small(group, BF16),
             small(group, BF16),
             small(group, BF16),
             small(group, BF16),
             sems((8,)), sems((8,)),
             sems((4, CHUNKS)), sems((4, CHUNKS)),
+            sems((2, CHUNKS)), sems((2, CHUNKS)),
             sems((2, CHUNKS)), sems((2, CHUNKS)),
             sems((CHUNKS,)), sems((CHUNKS,)),
             sems((CHUNKS,)), sems((CHUNKS,)),
@@ -398,6 +459,14 @@
         queries.reshape(tokens, feats), keys.reshape(tokens, feats), values.reshape(tokens, feats),
         w_in, out_grad.reshape(tokens, width), block_pattern, col_offset,
     )
+    outs = pl.pallas_call(
+        deliver,
+        out_shape=[jax.ShapeDtypeStruct(out.shape, out.dtype) for out in outs],
+        in_specs=[pl.BlockSpec(memory_space=pl.ANY)] * 5,
+        out_specs=[pl.BlockSpec(memory_space=pl.ANY)] * 5,
+        scratch_shapes=[sems((5, 4))],
+        cost_estimate=pl.CostEstimate(flops=0, bytes_accessed=11 * 2 ** 20, transcendentals=0),
+    )(*outs)
     layer_out, q_grad, k_grad, v_grad, w_grad = outs
     if not inside:
         w_grad = lax.psum_scatter(w_grad, ("dp", "seq"), scatter_dimension=0, tiled=True)

time: 158 us -> 309 us (1.96)
  the two profiles are of different devices: /device:TPU:26 before, /device:TPU:6 now
where the time goes in v1:
time: 309 us; the launch traced here: 307 us
  Pallas kernels  306 us (99%)
    pallas_call x1, Pallas kernels, shards(): pl.pallas_call(deliver, out_shape=[jax.ShapeDtypeStruct(out.shape, out.dt...  168 us
    pallas_call x1, Pallas kernels, shards(): pl.pallas_call(functools.partial(body, seq, inside), out_shape=[jax.Shape...  138 us

profile of v1, /device:TPU:6, one launch (start us, length us, event | category | flops | bytes accessed | tf_op | source)
XLA Modules:
  0.0 306.9 jit_solution(6575048943822135548)
XLA Ops:
  0.6 138.1 %shard_map.110 = (bf16[512,2048]{1,0:T(8,128)(2,1)}, bf16[512,1024]{1,0:T(8,128)(2,1)}, bf16[512,1024]{1,0:T(8,128)(2,1)}, bf16[512,1024]{1,0:T(8,128)(2,1)}, f32[32,2048]{1,0:T(8,128)}) custom-call(bf16[512,1024]{1,0:T(8,128)(2,1)} %bitcast.10, bf16[512,1024]{1,0:T(8,128)(2,1)} %bitcast.11, bf16[512,1024]{1,0:T(8,128)(2,1)} %bitcast.12, ...), custom_call_target="tpu_custom_call" | custom-call | flops 12000000000 | bytes 11534336 | tf_op jit(solution)/shard_map/pallas_call | solution.py:411
  138.7 168.0 %shard_map.111 = (bf16[512,2048]{1,0:T(8,128)(2,1)}, bf16[512,1024]{1,0:T(8,128)(2,1)}, bf16[512,1024]{1,0:T(8,128)(2,1)}, bf16[512,1024]{1,0:T(8,128)(2,1)}, f32[32,2048]{1,0:T(8,128)}) custom-call(bf16[512,2048]{1,0:T(8,128)(2,1)} %get-tuple-element.15.refs_0_, bf16[512,1024]{1,0:T(8,128)(2,1)} %get-tuple-element.16.refs_1_, ...), custom_call_target="tpu_custom_call" | custom-call | bytes 11534336 | tf_op jit(solution)/shard_map/pallas_call | solution.py:462

commit v2 on v1

--- a/solution.py
+++ b/solution.py
@@ -49,8 +49,8 @@
     return pl.ds(pl.multiple_of(head_idx * HD, HD), HD)
 
 
-def body(seq, inside, q_far, k_far, v_far, w_far, og_far, pattern, offset, lo, dq, dk, dv, wg,
-         q, k, v, w_in, og, l_sem, w_all, grads, att, att_t, col_in, col_src, col_bias, col_prob, p_scr, s_scr,
+def body(seq, inside, q_far, k_far, v_far, w_far, og_far, pattern, offset, lo_far, dq_far, dk_far, dv_far, wg,
+         q, k, v, w_in, og, l_sem, lo, row_grad, o_sem, w_all, grads, att, att_t, col_in, col_src, col_bias, col_prob, p_scr, s_scr,
          wp, core_in, y_src, y_in, keep, x_src, x_in, z_src, z_in,
          a_send, a_recv, g_send, g_recv, c_send, c_recv, y_send, y_recv, x_send, x_recv, z_send, z_recv):
     tokens = q.shape[0]
@@ -128,14 +128,14 @@
     row_at = lax.broadcasted_iota(jnp.int32, (tokens, tokens), 0)
     lane_at = lax.broadcasted_iota(jnp.int32, (tokens, tokens), 1)
 
-    def moved(tensor, head_idx, forth):
-        apart = (row_at - lane_at if forth else lane_at - row_at) - offset[head_idx]
+    def moved(tensor, head_idx):
+        apart = row_at - lane_at - offset[head_idx]
         chosen = jnp.where((apart == 0) | (apart == -tokens), 1.0, 0.0).astype(BF16)
         return nn(chosen, tensor).astype(BF16)
 
     def move_all(tensor, src_slot):
         for head_idx in range(HC):
-            shifted = moved(tensor[:, HALF + head_idx * HD:HALF + (head_idx + 1) * HD], head_idx, True)
+            shifted = moved(tensor[:, HALF + head_idx * HD:HALF + (head_idx + 1) * HD], head_idx)
             col_src[src_slot, :, :, head_idx * HD:(head_idx + 1) * HD] = shifted.reshape(seq, cols, HD)
 
     def spread_moved(src_slot, slot):
@@ -235,14 +235,15 @@
             half_prob = prob.astype(BF16)
             att[rows, where] = nn(half_prob, value).astype(BF16)
             score_grad = score_grads(prob, grads[rows, where], value)
-            dq[rows, where] = (nn(score_grad, key) * SCALE).astype(BF16)
+            row_grad[0, part * part_slots:(part + 1) * part_slots, :, where] = (
+                (nn(score_grad, key) * SCALE).astype(BF16).reshape(part_slots, cols, HD))
             p_scr[rows] = half_prob
             s_scr[rows] = score_grad
-        dk[:, where] = (tn(s_scr[...], q[:, where]) * SCALE).astype(BF16)
-        dv[:, where] = tn(p_scr[...], grads[:, where]).astype(BF16)
+        key_grad = (tn(s_scr[...], q[:, where]) * SCALE).astype(BF16)
+        value_grad = tn(p_scr[...], grads[:, where]).astype(BF16)
+        row_grad[1, :, :, where] = key_grad.reshape(seq, cols, HD)
+        row_grad[2, :, :, where] = value_grad.reshape(seq, cols, HD)
         return carry
-
-    lax.fori_loop(0, HR // 2, row_head, 0)
 
     def w_part(half):
         att_t[...] = att[:, half * HALF:(half + 1) * HALF].astype(F32).T.astype(BF16)
@@ -293,21 +294,34 @@
         value_grad = tn(p_scr[...], col_full(col_in, 3, where))
         col_src[4, :, :, where] = key_grad.astype(BF16).reshape(seq, cols, HD)
         col_src[5, :, :, where] = value_grad.astype(BF16).reshape(seq, cols, HD)
+
+        def one(step, inner):
+            peer = lax.rem(me + step, seq)
+            push(col_src.at[pl.ds(3, 3), peer, :, where], col_in.at[pl.ds(5, 3), me, :, where],
+                 a_send.at[5], a_recv.at[5], (dp, peer))
+            return inner
+
+        lax.fori_loop(1, seq, one, 0)
         return carry
 
     lax.fori_loop(0, HC, col_backward, 0)
 
     for slot in (5, 6, 7):
-        spread_moved(slot - 2, slot)
-    lax.fori_loop(HR // 2, HR, row_head, 0)
-    w_part(0)
-    if inside:
-        y_part(0)
+        col_in[slot, me] = col_src[slot - 2, me]
     arrived(4)
     att[:, HALF:] = col_in[4].reshape(tokens, HALF)
     w_part(1)
+    lax.fori_loop(0, HR, row_head, 0)
+    results = [
+        pltpu.make_async_copy(row_grad.at[at], far.at[:, :, pl.ds(0, HALF)], o_sem.at[at])
+        for at, far in enumerate((dq_far, dk_far, dv_far))]
+    for result in results:
+        result.start()
     if inside:
         y_part(1)
+    w_part(0)
+    if inside:
+        y_part(0)
 
         def x_step(c, carry):
             at = piece_cols(c)
@@ -326,6 +340,8 @@
         return carry
 
     lax.fori_loop(0, width // tall, layer, 0)
+    results.append(pltpu.make_async_copy(lo, lo_far, o_sem.at[6]))
+    results[-1].start()
 
     if inside:
         def z_step(c, carry):
@@ -347,14 +363,11 @@
 
         lax.fori_loop(0, CHUNKS, z_step, 0)
 
-    arrived(5)
-    dq[:, HALF:] = col_in[5].reshape(tokens, HALF)
-    for slot, target in ((6, dk), (7, dv)):
-        arrived(slot)
-        for head_idx in range(HC):
-            lanes = slice(head_idx * HD, (head_idx + 1) * HD)
-            back = moved(col_in[slot, :, :, lanes].reshape(tokens, HD), head_idx, False)
-            target[:, HALF + head_idx * HD:HALF + (head_idx + 1) * HD] = back
+    drain(col_in.at[pl.ds(5, 3), pl.ds(0, seq - 1)], a_recv.at[5])
+    for at, far in enumerate((dq_far, dk_far, dv_far)):
+        results.append(pltpu.make_async_copy(
+            col_in.at[5 + at], far.at[:, :, pl.ds(HALF, HALF)], o_sem.at[3 + at]))
+        results[-1].start()
 
     if inside:
         factor = (2 * seq * tokens) ** (-0.5)
@@ -372,23 +385,33 @@
                 drain(y_in.at[half, :, :, piece_cols(c)], y_send.at[half, c])
             drain(x_in.at[:, :, piece_cols(c)], x_send.at[c])
             drain(z_in.at[pl.ds(0, depth - 1), :, piece_cols(c)], z_send.at[c])
-    for slot in range(8):
+    for slot in range(5):
         drain(col_in.at[slot, pl.ds(0, seq - 1)], a_send.at[slot])
-
-
-def deliver(*refs):
-    sources, targets, sem = refs[:5], refs[5:10], refs[10]
-    copies = []
-    for at, (source, target) in enumerate(zip(sources, targets)):
-        cuts = 4 if source.shape[0] >= 64 else 1
-        rows = source.shape[0] // cuts
-        for cut in range(cuts):
-            part = pl.ds(cut * rows, rows)
-            copies.append(pltpu.make_async_copy(source.at[part], target.at[part], sem.at[at, cut]))
-    for copy in copies:
-        copy.start()
-    for copy in copies:
-        copy.wait()
+    drain(col_in.at[pl.ds(5, 3), pl.ds(0, seq - 1)], a_send.at[5])
+    for result in results:
+        result.wait()
+
+
+def deliver(offset, lo, dq, dk, dv, wg, lo_out, dq_out, dk_out, dv_out, wg_out):
+    head_idx = pl.program_id(0)
+    tokens = dk.shape[0]
+    lo_out[...] = lo[...]
+    dq_out[...] = dq[...]
+    wg_out[...] = wg[...]
+
+    @pl.when(head_idx < HR)
+    def _():
+        dk_out[...] = dk[...]
+        dv_out[...] = dv[...]
+
+    @pl.when(head_idx >= HR)
+    def _():
+        row_at = lax.broadcasted_iota(jnp.int32, (tokens, tokens), 0)
+        lane_at = lax.broadcasted_iota(jnp.int32, (tokens, tokens), 1)
+        apart = lane_at - row_at - offset[jnp.maximum(head_idx - HR, 0)]
+        chosen = jnp.where((apart == 0) | (apart == -tokens), 1.0, 0.0).astype(BF16)
+        dk_out[...] = nn(chosen, dk[...]).astype(BF16)
+        dv_out[...] = nn(chosen, dv[...]).astype(BF16)
 
 
 def shards(dp_count, seq, queries, keys, values, out_proj, out_grad, block_pattern, col_offset):
@@ -407,7 +430,7 @@
     sems = pltpu.SemaphoreType.DMA
     vmem = pl.BlockSpec(memory_space=pltpu.VMEM)
     smem = pl.BlockSpec(memory_space=pltpu.SMEM)
-    flat = jax.ShapeDtypeStruct((tokens, feats), BF16)
+    flat = jax.ShapeDtypeStruct((seq, cols, feats), BF16)
     outs = pl.pallas_call(
         functools.partial(body, seq, inside),
         out_shape=[
@@ -415,7 +438,7 @@
             jax.ShapeDtypeStruct((share if inside else feats, width), F32),
         ],
         in_specs=[pl.BlockSpec(memory_space=pl.ANY)] * 5 + [smem] * 2,
-        out_specs=[vmem] * 5,
+        out_specs=[pl.BlockSpec(memory_space=pl.ANY)] * 4 + [vmem],
         scratch_shapes=[
             pltpu.VMEM((tokens, feats), BF16),
             pltpu.VMEM((tokens, feats), BF16),
@@ -423,6 +446,9 @@
             pltpu.VMEM(w_in.shape, BF16),
             pltpu.VMEM((tokens, width), BF16),
             sems((5,)),
+            pltpu.VMEM((tokens, width), BF16),
+            pltpu.VMEM((3, seq, cols, HALF), BF16),
+            sems((7,)),
             small(split, BF16),
             pltpu.VMEM((tokens, feats), BF16),
             pltpu.VMEM((tokens, feats), BF16),
@@ -442,7 +468,7 @@
             small(group, BF16),
             small(group, BF16),
             small(group, BF16),
-            sems((8,)), sems((8,)),
+            sems((6,)), sems((6,)),
             sems((4, CHUNKS)), sems((4, CHUNKS)),
             sems((2, CHUNKS)), sems((2, CHUNKS)),
             sems((2, CHUNKS)), sems((2, CHUNKS)),
@@ -459,14 +485,19 @@
         queries.reshape(tokens, feats), keys.reshape(tokens, feats), values.reshape(tokens, feats),
         w_in, out_grad.reshape(tokens, width), block_pattern, col_offset,
     )
+    outs = [outs[0]] + [out.reshape(tokens, feats) for out in outs[1:4]] + [outs[4]]
+    lanes = [pl.BlockSpec((out.shape[0], out.shape[1] // (HR + HC)), lambda h: (0, h)) for out in outs]
     outs = pl.pallas_call(
         deliver,
+        grid=(HR + HC,),
         out_shape=[jax.ShapeDtypeStruct(out.shape, out.dtype) for out in outs],
-        in_specs=[pl.BlockSpec(memory_space=pl.ANY)] * 5,
-        out_specs=[pl.BlockSpec(memory_space=pl.ANY)] * 5,
-        scratch_shapes=[sems((5, 4))],
-        cost_estimate=pl.CostEstimate(flops=0, bytes_accessed=11 * 2 ** 20, transcendentals=0),
-    )(*outs)
+        in_specs=[smem] + lanes,
+        out_specs=lanes,
+        compiler_params=pltpu.CompilerParams(vmem_limit_bytes=32 * 2 ** 20),
+        cost_estimate=pl.CostEstimate(
+            flops=10 ** 9, bytes_accessed=11 * 2 ** 20, transcendentals=0
+        ),
+    )(col_offset, *outs)
     layer_out, q_grad, k_grad, v_grad, w_grad = outs
     if not inside:
         w_grad = lax.psum_scatter(w_grad, ("dp", "seq"), scatter_dimension=0, tiled=True)

time: 309 us -> 154 us (0.50)
  Pallas kernels: 306 us -> 147 us
  local copies, waits for them, and re-layouts: 0 us -> 6.21 us
    pallas_call x1, Pallas kernels: 168 us -> 6.11 us  [shards(): pl.pallas_call(deliver, grid=(HR + HC,), out_shape=[jax.ShapeDtypeStruct(...]
    unnamed x0 -> x12, local copies, waits for them, and re-layouts: none -> 6.21 us
where the time goes in v2:
time: 154 us
  Pallas kernels  147 us (95%)
  local copies, waits for them, and re-layouts  6.21 us (4%)
    pallas_call x1, Pallas kernels, shards(): pl.pallas_call(functools.partial(body, seq, inside), out_shape=[jax.Shape...  141 us
    unnamed x12, local copies, waits for them, and re-layouts  6.21 us
    pallas_call x1, Pallas kernels, shards(): pl.pallas_call(deliver, grid=(HR + HC,), out_shape=[jax.ShapeDtypeStruct(...  6.11 us

profile of v2, /device:TPU:6, one launch (start us, length us, event | category | flops | bytes accessed | tf_op | source)
XLA Modules:
  0.0 153.5 jit_solution(6661159655182753818)
XLA Ops:
  0.6 0.0 copy-start.5
  0.6 140.5 %shard_map.110 = (bf16[512,2048]{1,0:T(8,128)(2,1)}, bf16[16,32,1024]{2,1,0:T(8,128)(2,1)}, bf16[16,32,1024]{2,1,0:T(8,128)(2,1)}, bf16[16,32,1024]{2,1,0:T(8,128)(2,1)}, f32[32,2048]{1,0:T(8,128)}) custom-call(bf16[512,1024]{1,0:T(8,128)(2,1)} %bitcast.16, bf16[512,1024]{1,0:T(8,128)(2,1)} %bitcast.17, bf16[512,1024]{1,0:T(8,128)(2,1)} %bitcast.18, ...), custom_call_target="tpu_custom_call" | custom-call | flops 12000000000 | bytes 11534336 | tf_op jit(solution)/shard_map/pallas_call | solution.py:434
  141.2 0.0 copy-done.5
  141.2 0.0 copy-start
  141.2 1.6 %copy-done = bf16[512,2048]{1,0:T(8,128)(2,1)S(1)} copy-done((bf16[512,2048]{1,0:T(8,128)(2,1)S(1)}, bf16[512,2048]{1,0:T(8,128)(2,1)}, u32[]{:S(2)}) %copy-start) | copy-done | bytes 2097176
  142.8 0.0 copy-start.1
  142.8 1.2 copy-done.1
  144.0 0.0 copy-start.2
  144.0 1.2 copy-done.2
  145.2 0.0 copy-start.3
  145.2 1.2 copy-done.3
  146.5 0.0 copy-start.4
  146.5 0.9 copy-done.4
  147.4 6.1 %shard_map.111 = (bf16[512,2048]{1,0:T(8,128)(2,1)}, bf16[512,1024]{1,0:T(8,128)(2,1)}, bf16[512,1024]{1,0:T(8,128)(2,1)}, bf16[512,1024]{1,0:T(8,128)(2,1)}, f32[32,2048]{1,0:T(8,128)}) custom-call(s32[4]{0:T(128)S(1)} %copy-done.5, bf16[512,2048]{1,0:T(8,128)(2,1)S(1)} %copy-done, bf16[512,1024]{1,0:T(8,128)(2,1)S(1)} %bitcast.11, ...), custom_call_target="tpu_custom_call" | custom-call | flops 1000000000 | bytes 11534336 | tf_op jit(solution)/shard_map/pallas_call | solution.py:490
Async XLA Ops:
  0.6 140.6 %copy-start.5 = (s32[4]{0:T(128)S(1)}, s32[4]{0:T(128)}, u32[]{:S(2)}) copy-start(s32[4]{0:T(128)} %offset.3) | copy-start | bytes 52
  141.2 1.6 %copy-start = (bf16[512,2048]{1,0:T(8,128)(2,1)S(1)}, bf16[512,2048]{1,0:T(8,128)(2,1)}, u32[]{:S(2)}) copy-start(bf16[512,2048]{1,0:T(8,128)(2,1)} %get-tuple-element.15.lo) | copy-start | bytes 6291460
  142.8 1.2 copy-start.1
  144.0 1.2 copy-start.2
  145.2 1.2 copy-start.3
  146.5 0.9 copy-start.4

commit v3 on v2

--- a/solution.py
+++ b/solution.py
@@ -51,7 +51,7 @@
 
 def body(seq, inside, q_far, k_far, v_far, w_far, og_far, pattern, offset, lo_far, dq_far, dk_far, dv_far, wg,
          q, k, v, w_in, og, l_sem, lo, row_grad, o_sem, w_all, grads, att, att_t, col_in, col_src, col_bias, col_prob, p_scr, s_scr,
-         wp, core_in, y_src, y_in, keep, x_src, x_in, z_src, z_in,
+         wp, core_in, y_src, y_in, keep, x_src, x_in, z_src, z_in, z_keep, h_src, h_in,
          a_send, a_recv, g_send, g_recv, c_send, c_recv, y_send, y_recv, x_send, x_recv, z_send, z_recv):
     tokens = q.shape[0]
     cols = tokens // seq
@@ -63,7 +63,12 @@
     pair = me // 2
     y_at = lax.rem(pair, 2)
     z_at = pair // 2
-    depth = seq // 4
+    deep = seq // 8
+    lo_at = lax.rem(z_at, 2)
+    hi_at = z_at // 2
+
+    def device(hi_to, lo_to, y_to, core_to):
+        return (dp, ((hi_to * 2 + lo_to) * 2 + y_to) * 2 + core_to)
 
     near = [pltpu.make_async_copy(far, close, l_sem.at[at]) for at, (far, close) in enumerate(
         ((w_far, w_in), (k_far, k), (q_far, q), (v_far, v), (og_far, og)))]
@@ -111,16 +116,14 @@
 
     near[0].wait()
     if inside:
-        w_all[dp, z_at, y_at, core] = w_in[...]
-        for c in range(CHUNKS):
-            def z_step(step, carry, c=c):
-                z_to = lax.rem(z_at + step, depth)
-                block = w_all.at[dp, z_at, y_at, core, :, piece_cols(c)]
-                push(block, block, g_send.at[0, c], g_recv.at[0, c],
-                     (dp, (z_to * 2 + y_at) * 2 + core))
-                return carry
-
-            lax.fori_loop(1, depth, z_step, 0)
+        w_all[dp, hi_at, lo_at, y_at, core] = w_in[...]
+        for c in range(CHUNKS):
+            block = w_all.at[dp, hi_at, lo_at, y_at, core, :, piece_cols(c)]
+            push(block, block, g_send.at[4, c], g_recv.at[4, c], device(1 - hi_at, lo_at, y_at, core))
+        for c in range(CHUNKS):
+            drain(w_all.at[0, 0, 0, 0, 0, :, piece_cols(c)], g_recv.at[4, c])
+            block = w_all.at[dp, :, lo_at, y_at, core, :, piece_cols(c)]
+            push(block, block, g_send.at[0, c], g_recv.at[0, c], device(hi_at, 1 - lo_at, y_at, core))
         weights = w_all
     else:
         weights = w_in
@@ -151,8 +154,8 @@
 
     if inside:
         for c in range(CHUNKS):
-            drain(w_all.at[0, pl.ds(0, depth - 1), 0, 0, :, piece_cols(c)], g_recv.at[0, c])
-            block = w_all.at[dp, :, y_at, core, :, piece_cols(c)]
+            drain(w_all.at[0, :, 0, 0, 0, :, piece_cols(c)], g_recv.at[0, c])
+            block = w_all.at[dp, :, :, y_at, core, :, piece_cols(c)]
             push(block, block, g_send.at[1, c], g_recv.at[1, c],
                  (dp, (z_at * 2 + 1 - y_at) * 2 + core))
     near[2].wait()
@@ -163,21 +166,21 @@
     move_all(v, 1)
     if inside:
         for c in range(CHUNKS):
-            drain(w_all.at[0, :, 0, 0, :, piece_cols(c)], g_recv.at[1, c])
-            block = w_all.at[dp, :, :, core, :, piece_cols(c)]
+            drain(w_all.at[0, :, :, 0, 0, :, piece_cols(c)], g_recv.at[1, c])
+            block = w_all.at[dp, :, :, :, core, :, piece_cols(c)]
             push(block, block, g_send.at[2, c], g_recv.at[2, c], (1 - dp, me))
     spread_moved(1, 2)
     if inside:
         for c in range(CHUNKS):
-            drain(w_all.at[0, :, :, 0, :, piece_cols(c)], g_recv.at[2, c])
-            block = w_all.at[:, :, :, core, :, piece_cols(c)]
+            drain(w_all.at[0, :, :, :, 0, :, piece_cols(c)], g_recv.at[2, c])
+            block = w_all.at[:, :, :, :, core, :, piece_cols(c)]
             push(block, block, g_send.at[3, c], g_recv.at[3, c], (dp, pair * 2 + 1 - core))
         for c in range(CHUNKS):
-            drain(w_all.at[:, :, :, 0, :, piece_cols(c)], g_recv.at[3, c])
+            drain(w_all.at[:, :, :, :, 0, :, piece_cols(c)], g_recv.at[3, c])
     near[4].wait()
 
     tall = 256
-    steps = tall // (4 * weights.shape[4])
+    steps = tall // (8 * weights.shape[5])
 
     def attn_grad(half):
         def one(n, carry):
@@ -252,10 +255,10 @@
             at = piece_cols(c)
             product = nn(att_t[...], og[:, at])
             if inside:
-                wp[half, :, :, :, :, at] = product.astype(BF16).reshape(
-                    depth, 2, 2, HALF // seq, piece)
-                push(wp.at[half, :, :, 1 - core, :, at], core_in.at[half, :, :, :, at],
-                     c_send.at[half, c], c_recv.at[half, c], (dp, pair * 2 + 1 - core))
+                wp[half, :, :, :, :, :, at] = product.astype(BF16).reshape(
+                    deep, 2, 2, 2, HALF // seq, piece)
+                push(wp.at[half, :, :, :, 1 - core, :, at], core_in.at[half, :, :, :, :, at],
+                     c_send.at[half, c], c_recv.at[half, c], device(hi_at, lo_at, y_at, 1 - core))
             else:
                 wg[pl.ds(half * HALF, HALF), at] = product
             return carry
@@ -265,15 +268,16 @@
     def y_part(half):
         def one(c, carry):
             at = piece_cols(c)
-            drain(core_in.at[half, :, :, :, at], c_recv.at[half, c])
+            drain(core_in.at[half, :, :, :, :, at], c_recv.at[half, c])
             other = 1 - y_at
-            y_src[half, :, :, at] = (
-                wp[half, :, other, core, :, at].astype(F32) + core_in[half, :, other, :, at].astype(F32)
-            ).astype(BF16)
-            keep[half, :, :, at] = (
-                wp[half, :, y_at, core, :, at].astype(F32) + core_in[half, :, y_at, :, at].astype(F32))
-            push(y_src.at[half, :, :, at], y_in.at[half, :, :, at], y_send.at[half, c],
-                 y_recv.at[half, c], (dp, (z_at * 2 + other) * 2 + core))
+            y_src[half, :, :, :, at] = (
+                wp[half, :, :, other, core, :, at].astype(F32)
+                + core_in[half, :, :, other, :, at].astype(F32)).astype(BF16)
+            keep[half, :, :, :, at] = (
+                wp[half, :, :, y_at, core, :, at].astype(F32)
+                + core_in[half, :, :, y_at, :, at].astype(F32))
+            push(y_src.at[half, :, :, :, at], y_in.at[half, :, :, :, at], y_send.at[half, c],
+                 y_recv.at[half, c], device(hi_at, lo_at, other, core))
             return carry
 
         lax.fori_loop(0, CHUNKS, one, 0)
@@ -326,17 +330,17 @@
         def x_step(c, carry):
             at = piece_cols(c)
             for half in (0, 1):
-                drain(y_in.at[half, :, :, at], y_recv.at[half, c])
-            x_src[:, :, at] = (
-                keep[1 - dp, :, :, at] + y_in[1 - dp, :, :, at].astype(F32)).astype(BF16)
-            push(x_src.at[:, :, at], x_in.at[:, :, at], x_send.at[c], x_recv.at[c], (1 - dp, me))
+                drain(y_in.at[half, :, :, :, at], y_recv.at[half, c])
+            x_src[:, :, :, at] = (
+                keep[1 - dp, :, :, :, at] + y_in[1 - dp, :, :, :, at].astype(F32)).astype(BF16)
+            push(x_src.at[:, :, :, at], x_in.at[:, :, :, at], x_send.at[c], x_recv.at[c], (1 - dp, me))
             return carry
 
         lax.fori_loop(0, CHUNKS, x_step, 0)
 
     def layer(n, carry):
         at = pl.ds(pl.multiple_of(n * tall, tall), tall)
-        lo[:, at] = nn(att[...], weights[:, :, :, :, :, at].reshape(2 * HALF, tall)).astype(BF16)
+        lo[:, at] = nn(att[...], weights[:, :, :, :, :, :, at].reshape(2 * HALF, tall)).astype(BF16)
         return carry
 
     lax.fori_loop(0, width // tall, layer, 0)
@@ -346,22 +350,31 @@
     if inside:
         def z_step(c, carry):
             at = piece_cols(c)
-            drain(x_in.at[:, :, at], x_recv.at[c])
-            z_src[:, :, at] = (
-                keep[dp, :, :, at] + y_in[dp, :, :, at].astype(F32) + x_in[:, :, at].astype(F32)
-            ).astype(BF16)
-            z_in[z_at, :, at] = z_src[z_at, :, at]
-
-            def one(step, inner):
-                peer = lax.rem(z_at + step, depth)
-                push(z_src.at[peer, :, at], z_in.at[z_at, :, at], z_send.at[c], z_recv.at[c],
-                     (dp, (peer * 2 + y_at) * 2 + core))
-                return inner
-
-            lax.fori_loop(1, depth, one, 0)
+            drain(x_in.at[:, :, :, at], x_recv.at[c])
+
+            def total(which):
+                return (keep[dp, :, which, :, at] + y_in[dp, :, which, :, at].astype(F32)
+                        + x_in[:, which, :, at].astype(F32))
+
+            z_src[:, :, at] = total(1 - lo_at).astype(BF16)
+            z_keep[:, :, at] = total(lo_at)
+            push(z_src.at[:, :, at], z_in.at[:, :, at], z_send.at[0, c], z_recv.at[0, c],
+                 device(hi_at, 1 - lo_at, y_at, core))
             return carry
 
         lax.fori_loop(0, CHUNKS, z_step, 0)
+
+        def h_step(c, carry):
+            at = piece_cols(c)
+            drain(z_in.at[:, :, at], z_recv.at[0, c])
+            other = 1 - hi_at
+            h_src[:, at] = (z_keep[other, :, at] + z_in[other, :, at].astype(F32)).astype(BF16)
+            wg[:, at] = z_keep[hi_at, :, at] + z_in[hi_at, :, at].astype(F32)
+            push(h_src.at[:, at], h_in.at[:, at], z_send.at[1, c], z_recv.at[1, c],
+                 device(other, lo_at, y_at, core))
+            return carry
+
+        lax.fori_loop(0, CHUNKS, h_step, 0)
 
     drain(col_in.at[pl.ds(5, 3), pl.ds(0, seq - 1)], a_recv.at[5])
     for at, far in enumerate((dq_far, dk_far, dv_far)):
@@ -373,18 +386,20 @@
         factor = (2 * seq * tokens) ** (-0.5)
         for c in range(CHUNKS):
             at = piece_cols(c)
-            drain(z_in.at[pl.ds(0, depth - 1), :, at], z_recv.at[c])
-            wg[:, at] = jnp.sum(z_in[:, :, at].astype(F32), axis=0) * factor
-        for c in range(CHUNKS):
-            drain(w_all.at[0, pl.ds(0, depth - 1), 0, 0, :, piece_cols(c)], g_send.at[0, c])
-            drain(w_all.at[0, :, 0, 0, :, piece_cols(c)], g_send.at[1, c])
-            drain(w_all.at[0, :, :, 0, :, piece_cols(c)], g_send.at[2, c])
-            drain(w_all.at[:, :, :, 0, :, piece_cols(c)], g_send.at[3, c])
+            drain(h_in.at[:, at], z_recv.at[1, c])
+            wg[:, at] = (wg[:, at] + h_in[:, at].astype(F32)) * factor
+        for c in range(CHUNKS):
+            drain(w_all.at[0, :, 0, 0, 0, :, piece_cols(c)], g_send.at[0, c])
+            drain(w_all.at[0, :, :, 0, 0, :, piece_cols(c)], g_send.at[1, c])
+            drain(w_all.at[0, :, :, :, 0, :, piece_cols(c)], g_send.at[2, c])
+            drain(w_all.at[:, :, :, :, 0, :, piece_cols(c)], g_send.at[3, c])
             for half in (0, 1):
-                drain(core_in.at[half, :, :, :, piece_cols(c)], c_send.at[half, c])
-                drain(y_in.at[half, :, :, piece_cols(c)], y_send.at[half, c])
-            drain(x_in.at[:, :, piece_cols(c)], x_send.at[c])
-            drain(z_in.at[pl.ds(0, depth - 1), :, piece_cols(c)], z_send.at[c])
+                drain(core_in.at[half, :, :, :, :, piece_cols(c)], c_send.at[half, c])
+                drain(y_in.at[half, :, :, :, piece_cols(c)], y_send.at[half, c])
+            drain(x_in.at[:, :, :, piece_cols(c)], x_send.at[c])
+            drain(z_in.at[:, :, piece_cols(c)], z_send.at[0, c])
+            drain(h_in.at[:, piece_cols(c)], z_send.at[1, c])
+            drain(w_all.at[0, 0, 0, 0, 0, :, piece_cols(c)], g_send.at[4, c])
     for slot in range(5):
         drain(col_in.at[slot, pl.ds(0, seq - 1)], a_send.at[slot])
     drain(col_in.at[pl.ds(5, 3), pl.ds(0, seq - 1)], a_send.at[5])
@@ -419,14 +434,14 @@
     width = out_grad.shape[3]
     share = out_proj.shape[0]
     cols = tokens // seq
-    inside = dp_count == 2 and share % 16 == 0
-    split = (2, seq // 4, 2, 2, feats // (2 * seq), width)
+    inside = dp_count == 2 and seq == 16 and share % 16 == 0
+    split = (2, seq // 8, 2, 2, 2, feats // (2 * seq), width)
     if inside:
         w_in = out_proj
     else:
         w_in = lax.all_gather(out_proj, ("dp", "seq"), axis=0, tiled=True).reshape(split)
     small = lambda shape, kind: pltpu.VMEM(shape if inside else (16, 128), kind)
-    group = (seq // 4, share, width)
+    group = (seq // 8, 2, share, width)
     sems = pltpu.SemaphoreType.DMA
     vmem = pl.BlockSpec(memory_space=pltpu.VMEM)
     smem = pl.BlockSpec(memory_space=pltpu.SMEM)
@@ -459,21 +474,24 @@
             pltpu.VMEM((HC, tokens, tokens), F32),
             pltpu.VMEM((tokens, tokens), BF16),
             pltpu.VMEM((tokens, tokens), BF16),
-            small((2, seq // 4, 2, 2, share, width), BF16),
-            small((2, seq // 4, 2, share, width), BF16),
+            small((2, seq // 8, 2, 2, 2, share, width), BF16),
+            small((2, seq // 8, 2, 2, share, width), BF16),
             small((2,) + group, BF16),
             small((2,) + group, BF16),
             small((2,) + group, F32),
             small(group, BF16),
             small(group, BF16),
-            small(group, BF16),
-            small(group, BF16),
+            small((2, share, width), BF16),
+            small((2, share, width), BF16),
+            small((2, share, width), F32),
+            small((share, width), BF16),
+            small((share, width), BF16),
             sems((6,)), sems((6,)),
-            sems((4, CHUNKS)), sems((4, CHUNKS)),
+            sems((5, CHUNKS)), sems((5, CHUNKS)),
             sems((2, CHUNKS)), sems((2, CHUNKS)),
             sems((2, CHUNKS)), sems((2, CHUNKS)),
             sems((CHUNKS,)), sems((CHUNKS,)),
-            sems((CHUNKS,)), sems((CHUNKS,)),
+            sems((2, CHUNKS)), sems((2, CHUNKS)),
         ],
         compiler_params=pltpu.CompilerParams(
             collective_id=0, has_side_effects=True, vmem_limit_bytes=58 * 2 ** 20
@@ -493,7 +511,7 @@
         out_shape=[jax.ShapeDtypeStruct(out.shape, out.dtype) for out in outs],
         in_specs=[smem] + lanes,
         out_specs=lanes,
-        compiler_params=pltpu.CompilerParams(vmem_limit_bytes=32 * 2 ** 20),
+        compiler_params=pltpu.CompilerParams(vmem_limit_bytes=60 * 2 ** 20),
         cost_estimate=pl.CostEstimate(
             flops=10 ** 9, bytes_accessed=11 * 2 ** 20, transcendentals=0
         ),

time: 154 us -> 151 us (0.981)
  local copies, waits for them, and re-layouts: 6.21 us -> 0 us
  Pallas kernels: 147 us -> 150 us
    unnamed x12 -> x0, local copies, waits for them, and re-layouts: 6.21 us -> none
    pallas_call x1, Pallas kernels: 6.11 us -> 8.3 us  [shards(): pl.pallas_call(deliver, grid=(HR + HC,), out_shape=[jax.ShapeDtypeStruct(...]
where the time goes in v3:
time: 151 us; the launch traced here: 150 us
  Pallas kernels  150 us (99%)
    pallas_call x1, Pallas kernels, shards(): pl.pallas_call(functools.partial(body, seq, inside), out_shape=[jax.Shape...  141 us
    pallas_call x1, Pallas kernels, shards(): pl.pallas_call(deliver, grid=(HR + HC,), out_shape=[jax.ShapeDtypeStruct(...  8.3 us

profile of v3, /device:TPU:6, one launch (start us, length us, event | category | flops | bytes accessed | tf_op | source)
XLA Modules:
  0.0 150.3 jit_solution(6569310105705075168)
XLA Ops:
  0.6 141.4 %shard_map.110 = (bf16[512,2048]{1,0:T(8,128)(2,1)}, bf16[16,32,1024]{2,1,0:T(8,128)(2,1)}, bf16[16,32,1024]{2,1,0:T(8,128)(2,1)}, bf16[16,32,1024]{2,1,0:T(8,128)(2,1)}, f32[32,2048]{1,0:T(8,128)}) custom-call(bf16[512,1024]{1,0:T(8,128)(2,1)} %bitcast.16, bf16[512,1024]{1,0:T(8,128)(2,1)} %bitcast.17, bf16[512,1024]{1,0:T(8,128)(2,1)} %bitcast.18, ...), custom_call_target="tpu_custom_call" | custom-call | flops 12000000000 | bytes 11534336 | tf_op jit(solution)/shard_map/pallas_call | solution.py:449
  142.0 8.3 %shard_map.111 = (bf16[512,2048]{1,0:T(8,128)(2,1)}, bf16[512,1024]{1,0:T(8,128)(2,1)}, bf16[512,1024]{1,0:T(8,128)(2,1)}, bf16[512,1024]{1,0:T(8,128)(2,1)}, f32[32,2048]{1,0:T(8,128)}) custom-call(s32[4]{0:T(128)} %offset.3, bf16[512,2048]{1,0:T(8,128)(2,1)} %get-tuple-element.15.lo, bf16[512,1024]{1,0:T(8,128)(2,1)} %bitcast.11, ...), custom_call_target="tpu_custom_call" | custom-call | flops 1000000000 | bytes 11534336 | tf_op jit(solution)/shard_map/pallas_call | solution.py:508

commit v4 on v3

--- a/solution.py
+++ b/solution.py
@@ -50,7 +50,7 @@
 
 
 def body(seq, inside, q_far, k_far, v_far, w_far, og_far, pattern, offset, lo_far, dq_far, dk_far, dv_far, wg,
-         q, k, v, w_in, og, l_sem, lo, row_grad, o_sem, w_all, grads, att, att_t, col_in, col_src, col_bias, col_prob, p_scr, s_scr,
+         q, k, v, w_in, og, l_sem, lo, row_grad, back, o_sem, w_all, grads, att, att_t, col_in, col_src, col_bias, col_prob, p_scr, s_scr,
          wp, core_in, y_src, y_in, keep, x_src, x_in, z_src, z_in, z_keep, h_src, h_in,
          a_send, a_recv, g_send, g_recv, c_send, c_recv, y_send, y_recv, x_send, x_recv, z_send, z_recv):
     tokens = q.shape[0]
@@ -131,14 +131,14 @@
     row_at = lax.broadcasted_iota(jnp.int32, (tokens, tokens), 0)
     lane_at = lax.broadcasted_iota(jnp.int32, (tokens, tokens), 1)
 
-    def moved(tensor, head_idx):
-        apart = row_at - lane_at - offset[head_idx]
+    def moved(tensor, head_idx, forth):
+        apart = (row_at - lane_at if forth else lane_at - row_at) - offset[head_idx]
         chosen = jnp.where((apart == 0) | (apart == -tokens), 1.0, 0.0).astype(BF16)
         return nn(chosen, tensor).astype(BF16)
 
     def move_all(tensor, src_slot):
         for head_idx in range(HC):
-            shifted = moved(tensor[:, HALF + head_idx * HD:HALF + (head_idx + 1) * HD], head_idx)
+            shifted = moved(tensor[:, HALF + head_idx * HD:HALF + (head_idx + 1) * HD], head_idx, True)
             col_src[src_slot, :, :, head_idx * HD:(head_idx + 1) * HD] = shifted.reshape(seq, cols, HD)
 
     def spread_moved(src_slot, slot):
@@ -378,8 +378,14 @@
 
     drain(col_in.at[pl.ds(5, 3), pl.ds(0, seq - 1)], a_recv.at[5])
     for at, far in enumerate((dq_far, dk_far, dv_far)):
+        if at > 0:
+            for head_idx in range(HC):
+                lanes = slice(head_idx * HD, (head_idx + 1) * HD)
+                home = moved(col_in[5 + at, :, :, lanes].reshape(tokens, HD), head_idx, False)
+                back[at - 1, :, :, lanes] = home.reshape(seq, cols, HD)
         results.append(pltpu.make_async_copy(
-            col_in.at[5 + at], far.at[:, :, pl.ds(HALF, HALF)], o_sem.at[3 + at]))
+            back.at[at - 1] if at > 0 else col_in.at[5],
+            far.at[:, :, pl.ds(HALF, HALF)], o_sem.at[3 + at]))
         results[-1].start()
 
     if inside:
@@ -407,26 +413,9 @@
         result.wait()
 
 
-def deliver(offset, lo, dq, dk, dv, wg, lo_out, dq_out, dk_out, dv_out, wg_out):
-    head_idx = pl.program_id(0)
-    tokens = dk.shape[0]
-    lo_out[...] = lo[...]
-    dq_out[...] = dq[...]
-    wg_out[...] = wg[...]
-
-    @pl.when(head_idx < HR)
-    def _():
-        dk_out[...] = dk[...]
-        dv_out[...] = dv[...]
-
-    @pl.when(head_idx >= HR)
-    def _():
-        row_at = lax.broadcasted_iota(jnp.int32, (tokens, tokens), 0)
-        lane_at = lax.broadcasted_iota(jnp.int32, (tokens, tokens), 1)
-        apart = lane_at - row_at - offset[jnp.maximum(head_idx - HR, 0)]
-        chosen = jnp.where((apart == 0) | (apart == -tokens), 1.0, 0.0).astype(BF16)
-        dk_out[...] = nn(chosen, dk[...]).astype(BF16)
-        dv_out[...] = nn(chosen, dv[...]).astype(BF16)
+def deliver(*refs):
+    for source, target in zip(refs[:5], refs[5:]):
+        target[...] = source[...]
 
 
 def shards(dp_count, seq, queries, keys, values, out_proj, out_grad, block_pattern, col_offset):
@@ -463,6 +452,7 @@
             sems((5,)),
             pltpu.VMEM((tokens, width), BF16),
             pltpu.VMEM((3, seq, cols, HALF), BF16),
+            pltpu.VMEM((2, seq, cols, HALF), BF16),
             sems((7,)),
             small(split, BF16),
             pltpu.VMEM((tokens, feats), BF16),
@@ -504,18 +494,18 @@
         w_in, out_grad.reshape(tokens, width), block_pattern, col_offset,
     )
     outs = [outs[0]] + [out.reshape(tokens, feats) for out in outs[1:4]] + [outs[4]]
-    lanes = [pl.BlockSpec((out.shape[0], out.shape[1] // (HR + HC)), lambda h: (0, h)) for out in outs]
+    blocks = [pl.BlockSpec((out.shape[0] // 4, out.shape[1]), lambda n: (n, 0)) for out in outs]
     outs = pl.pallas_call(
         deliver,
-        grid=(HR + HC,),
+        grid=(4,),
         out_shape=[jax.ShapeDtypeStruct(out.shape, out.dtype) for out in outs],
-        in_specs=[smem] + lanes,
-        out_specs=lanes,
+        in_specs=blocks,
+        out_specs=blocks,
         compiler_params=pltpu.CompilerParams(vmem_limit_bytes=60 * 2 ** 20),
         cost_estimate=pl.CostEstimate(
-            flops=10 ** 9, bytes_accessed=11 * 2 ** 20, transcendentals=0
+            flops=0, bytes_accessed=11 * 2 ** 20, transcendentals=0
         ),
-    )(col_offset, *outs)
+    )(*outs)
     layer_out, q_grad, k_grad, v_grad, w_grad = outs
     if not inside:
         w_grad = lax.psum_scatter(w_grad, ("dp", "seq"), scatter_dimension=0, tiled=True)

time: 151 us -> 148 us (0.980)
  Pallas kernels: 150 us -> 147 us
    pallas_call x1, Pallas kernels: 8.3 us -> 5.34 us  [shards(): pl.pallas_call(deliver, grid=(4,), out_shape=[jax.ShapeDtypeStruct(out.sh...]
where the time goes in v4:
time: 148 us; the launch traced here: 147 us
  Pallas kernels  147 us (99%)
    pallas_call x1, Pallas kernels, shards(): pl.pallas_call(functools.partial(body, seq, inside), out_shape=[jax.Shape...  141 us
    pallas_call x1, Pallas kernels, shards(): pl.pallas_call(deliver, grid=(4,), out_shape=[jax.ShapeDtypeStruct(out.sh...  5.34 us

profile of v4, /device:TPU:6, one launch (start us, length us, event | category | flops | bytes accessed | tf_op | source)
XLA Modules:
  0.0 147.3 jit_solution(13055163731013516713)
XLA Ops:
  0.6 141.4 %shard_map.110 = (bf16[512,2048]{1,0:T(8,128)(2,1)}, bf16[16,32,1024]{2,1,0:T(8,128)(2,1)}, bf16[16,32,1024]{2,1,0:T(8,128)(2,1)}, bf16[16,32,1024]{2,1,0:T(8,128)(2,1)}, f32[32,2048]{1,0:T(8,128)}) custom-call(bf16[512,1024]{1,0:T(8,128)(2,1)} %bitcast.16, bf16[512,1024]{1,0:T(8,128)(2,1)} %bitcast.17, bf16[512,1024]{1,0:T(8,128)(2,1)} %bitcast.18, ...), custom_call_target="tpu_custom_call" | custom-call | flops 12000000000 | bytes 11534336 | tf_op jit(solution)/shard_map/pallas_call | solution.py:438
  142.0 5.3 %shard_map.111 = (bf16[512,2048]{1,0:T(8,128)(2,1)}, bf16[512,1024]{1,0:T(8,128)(2,1)}, bf16[512,1024]{1,0:T(8,128)(2,1)}, bf16[512,1024]{1,0:T(8,128)(2,1)}, f32[32,2048]{1,0:T(8,128)}) custom-call(bf16[512,2048]{1,0:T(8,128)(2,1)} %get-tuple-element.15.refs_0_, bf16[512,1024]{1,0:T(8,128)(2,1)} %bitcast.11, bf16[512,1024]{1,0:T(8,128)(2,1)} %bitcast.12, ...), custom_call_target="tpu_custom_call" | custom-call | bytes 11534336 | tf_op jit(solution)/shard_map/pallas_call | solution.py:498
